TPU v7x, 32 devices: a whole 2x2x4 slice. The times are simulated.
32 devices in a mesh: sec: 2 (over y), row: 4 (over x, core), col: 4 (over z).
Axes of the slice: x: 2, y: 2, z: 4, core: 2. Of those that a mesh axis runs over, the one named last changes fastest.
Arguments:
- sketch: float32 [32, 64, 2048], P(None, ('sec', 'row'), 'col'), parts along dimension 1, may hold values from -6 to 6
- weights: float32 [8, 64, 2048], P(None, ('sec', 'row'), 'col'), parts along dimension 1, may hold values from 0.05 to 1
Outputs:
- basis: float32 [32, 64, 2048], P(None, ('sec', 'row'), 'col'), parts along dimension 1
- factor: float32 [64, 32], P('sec'), parts along dimension 0
There are 2 independent parts, one for each index of `sec`. A program takes and returns all parts, laid end to end along the dimension named above; each array names one. Nothing has to cross between parts.
All inputs are finite; a program needn't handle non-finite values.
Results may differ from a plain program's by a relative error of at most 0.0001.
Values sent between devices are 32-bit elements; how exact they have to be, the bound alone decides.
A program may use at most 64 MiB of HBM per device.

v0:
```python
import jax
import jax.numpy as jnp
from jax import lax
from jax.sharding import PartitionSpec as P

ITERS = 2
NEIGHBOURS = ((-1, -1), (-1, 0), (-1, 1), (0, -1), (0, 1), (1, -1), (1, 0), (1, 1))


def padded_2(block, sides, width):
    for axis, dim in sides:
        count = lax.axis_size(axis)
        forward = [(i, i + 1) for i in range(count - 1)]
        backward = [(target, source) for source, target in forward]
        low = lax.ppermute(
            lax.slice_in_dim(block, block.shape[dim] - width, None, axis=dim), axis, forward
        )
        high = lax.ppermute(lax.slice_in_dim(block, 0, width, axis=dim), axis, backward)
        block = jnp.concatenate([low, block, high], axis=dim)
    return block


def stencil(padded, local_weights):
    height = local_weights.shape[1]
    breadth = local_weights.shape[2]
    centre = padded[:, 1 : 1 + height, 1 : 1 + breadth]
    summed = jnp.sum(local_weights, axis=0) * centre
    for position, offset in enumerate(NEIGHBOURS):
        shift_row = offset[0]
        shift_col = offset[1]
        summed = (
            summed
            + local_weights[position]
            * padded[
                :, 1 + shift_row : 1 + shift_row + height, 1 + shift_col : 1 + shift_col + breadth
            ]
        )
    return summed


def factorize(interior, pixel_count):
    columns = interior.shape[0]
    flattened = interior.reshape(columns, -1)
    gram_local = jnp.dot(flattened, flattened.T, precision=lax.Precision.HIGHEST) / pixel_count
    summed = lax.psum(gram_local, ("row", "col"))
    return jnp.linalg.cholesky(summed)


def solve_planes(lower_tri, image_vals):
    columns = image_vals.shape[0]
    solved = jax.scipy.linalg.solve_triangular(
        lower_tri, image_vals.reshape(columns, -1), lower=True
    )
    return solved.reshape(image_vals.shape)


def on_device(sketch, weights):
    tile_rows = sketch.shape[1]
    tile_cols = sketch.shape[2]
    pixel_count = tile_rows * tile_cols * lax.axis_size("row") * lax.axis_size("col")
    wide_weights = padded_2(weights, (("row", 1), ("col", 2)), ITERS - 1)
    sketch_field = padded_2(sketch, (("row", 1), ("col", 2)), ITERS)
    for power_step in range(ITERS):
        margin = ITERS - 1 - power_step
        local_weights = wide_weights[
            :,
            power_step : power_step + tile_rows + 2 * margin,
            power_step : power_step + tile_cols + 2 * margin,
        ]
        image_vals = stencil(sketch_field, local_weights)
        interior = image_vals[:, margin : margin + tile_rows, margin : margin + tile_cols]
        lower_tri = factorize(interior, pixel_count)
        sketch_field = solve_planes(lower_tri, image_vals)
    return (sketch_field, lower_tri.T)


def solution(mesh):
    return jax.shard_map(
        on_device,
        mesh=mesh,
        in_specs=(P(None, ("sec", "row"), "col"), P(None, ("sec", "row"), "col")),
        out_specs=(P(None, ("sec", "row"), "col"), P("sec", None)),
        check_vma=False,
    )
```

profile of v0, /device:TPU:0, one launch (start us, length us, event | category | flops | bytes accessed | tf_op | source)
XLA Modules:
  0.0 178.7 jit_solution(1603129696953447877)
XLA Ops:
  0.6 1.1 fusion.45
  1.7 2.4 %collective-permute-start = (f32[8,1,512]{2,1,0:T(1,128)S(1)}, f32[8,1,512]{2,1,0:T(1,128)S(1)}, u32[]{:S(2)}, u32[]{:S(2)}) collective-permute-start(f32[8,1,512]{2,1,0:T(1,128)S(1)} %get-tuple-element.31), channel_id=1, source_target_pairs={{0,4},{4,8},{8,12},{1,5},{5,9},{9,13},{2,6},{6,10},{10,14},{3,7},{... | collective-permute-start | bytes 49160 | tf_op jit(solution)/shard_map/ppermute | solution.py:15
  4.1 1.4 collective-permute-start.1
  5.5 1.4 fusion.44
  6.9 5.1 %collective-permute-start.4 = (f32[32,2,512]{2,0,1:T(8,128)S(1)}, f32[32,2,512]{2,0,1:T(8,128)S(1)}, u32[]{:S(2)}, u32[]{:S(2)}) collective-permute-start(f32[32,2,512]{2,0,1:T(8,128)S(1)} %copy.47), channel_id=1, source_target_pairs={{0,4},{4,8},{8,12},{1,5},{5,9},{9,13},{2,6},{6,10},{10,14},{3,7},{... | collective-permute-start | bytes 393224 | tf_op jit(solution)/shard_map/ppermute | solution.py:15
  12.1 1.3 collective-permute-start.5
  13.4 0.9 pad_maximum_fusion.6
  14.3 3.5 %collective-permute-start.2 = (f32[8,10,1]{2,1,0:T(8,128)S(1)}, f32[8,10,1]{2,1,0:T(8,128)S(1)}, u32[]{:S(2)}, u32[]{:S(2)}) collective-permute-start(f32[8,10,1]{2,1,0:T(8,128)S(1)} %get-tuple-element.21), channel_id=1, source_target_pairs={{0,1},{1,2},{2,3},{4,5},{5,6},{6,7},{8,9},{9,10},{10,11},{12,13},{... | collective-permute-start | bytes 968 | tf_op jit(solution)/shard_map/ppermute | solution.py:15
  17.8 1.3 collective-permute-start.3
  19.2 0.5 collective-permute-done.2
  19.7 4.3 %collective-permute-done.3 = f32[8,10,1]{2,1,0:T(8,128)S(1)} collective-permute-done((f32[8,10,1]{2,1,0:T(8,128)S(1)}, f32[8,10,1]{2,1,0:T(8,128)S(1)}, u32[]{:S(2)}, u32[]{:S(2)}) %collective-permute-start.3) | collective-permute-done | bytes 352 | tf_op jit(solution)/shard_map/ppermute | solution.py:18
  24.8 3.5 %collective-permute-start.6 = (f32[32,12,2]{2,0,1:T(8,128)S(1)}, f32[32,12,2]{2,0,1:T(8,128)S(1)}, u32[]{:S(2)}, u32[]{:S(2)}) collective-permute-start(f32[32,12,2]{2,0,1:T(8,128)S(1)} %get-tuple-element.7), channel_id=1, source_target_pairs={{0,1},{1,2},{2,3},{4,5},{5,6},{6,7},{8,9},{9,10},{10,11},{12,13},{... | collective-permute-start | bytes 9224 | tf_op jit(solution)/shard_map/ppermute | solution.py:15
  28.3 1.3 collective-permute-start.7
  29.6 3.9 %collective-permute-done.6 = f32[32,12,2]{2,0,1:T(8,128)S(1)} collective-permute-done((f32[32,12,2]{2,0,1:T(8,128)S(1)}, f32[32,12,2]{2,0,1:T(8,128)S(1)}, u32[]{:S(2)}, u32[]{:S(2)}) %collective-permute-start.6) | collective-permute-done | bytes 3104 | tf_op jit(solution)/shard_map/ppermute | solution.py:15
  33.5 4.1 %collective-permute-done.7 = f32[32,12,2]{2,0,1:T(8,128)S(1)} collective-permute-done((f32[32,12,2]{2,0,1:T(8,128)S(1)}, f32[32,12,2]{2,0,1:T(8,128)S(1)}, u32[]{:S(2)}, u32[]{:S(2)}) %collective-permute-start.7) | collective-permute-done | bytes 3104 | tf_op jit(solution)/shard_map/ppermute | solution.py:18
  38.0 1.4 fusion.7
  39.4 0.7 fusion.1
  40.6 59.4 %psum.14 = f32[32,32]{0,1:T(8,128)S(1)} all-reduce(f32[32,32]{0,1:T(8,128)S(1)} %fusion.1), channel_id=1, replica_groups=mesh['sec'=2,'row'=4,'col'=4] {'row','col'}, use_global_device_ids=true, to_apply=%region_2.3 | all-reduce | flops 1024 | bytes 8192 | tf_op jit(solution)/shard_map/psum | solution.py:45
  100.1 2.9 %cholesky.44 = f32[32,32]{1,0:T(8,128)S(1)} custom-call(f32[32,32]{1,0:T(8,128)S(1)} %fusion.38), custom_call_target="Cholesky" | custom-call | tf_op jit(solution)/shard_map/jit(cholesky)/cholesky | solution.py:46
  103.1 0.6 compare_reduce_fusion.1
  103.7 0.7 fusion.34
  104.4 2.4 %custom-call.10 = f32[1,32,32]{1,2,0:T(8,128)S(1)} custom-call(f32[1,32,32]{2,1,0:T(8,128)S(1)} %fusion.34), custom_call_target="InvertDiagBlocksLowerTriangular" | custom-call | tf_op jit(solution)/shard_map/jit(_solve_triangular)/triangular_solve | solution.py:51
  107.7 1.0 fusion.20
  108.7 2.1 %fusion = f32[32,32]{0,1:T(8,128)S(1)} fusion(f32[32,10,514]{2,0,1:T(8,128)S(1)} %fusion.20, f32[8,512]{1,0:T(8,128)S(1)} %get-tuple-element.29, f32[8,512]{1,0:T(8,128)S(1)} %get-tuple-element.30, f32[8,512]{1,0:T(8,128)S(1)} %get-tuple-element.24, f32[8,512]{1,0:T(8,128)S(1)} %get-tuple-element.25, f32[8,512]{1,0:T(8,128)S(1)} %get-tuple-element.26, ...), kind=kOutput, calls=%fused_computation.5 | convolution fusion | flops 54789120 | bytes 9736192 | tf_op jit(solution)/shard_map/dot_general | solution.py:44
  110.8 58.0 %psum.15 = f32[32,32]{0,1:T(8,128)S(1)} all-reduce(f32[32,32]{0,1:T(8,128)S(1)} %fusion), channel_id=1, replica_groups=mesh['sec'=2,'row'=4,'col'=4] {'row','col'}, use_global_device_ids=true, to_apply=%region_5.7 | all-reduce | flops 1024 | bytes 8192 | tf_op jit(solution)/shard_map/psum | solution.py:45
  168.8 2.9 %cholesky.55 = f32[32,32]{1,0:T(8,128)S(1)} custom-call(f32[32,32]{1,0:T(8,128)S(1)} %fusion.37), custom_call_target="Cholesky" | custom-call | tf_op jit(solution)/shard_map/jit(cholesky)/cholesky | solution.py:46
  171.7 0.6 compare_reduce_fusion
  172.4 0.7 fusion.41
  173.0 2.4 %custom-call.11 = f32[1,32,32]{1,2,0:T(8,128)S(1)} custom-call(f32[1,32,32]{2,1,0:T(8,128)S(1)} %get-tuple-element.34), custom_call_target="InvertDiagBlocksLowerTriangular" | custom-call | tf_op jit(solution)/shard_map/jit(_solve_triangular)/triangular_solve | solution.py:51
  175.5 1.4 fusion.22
  176.9 1.1 copy.28
  178.0 0.7 copy.29
  (28 shorter events, 2.8 us)
Async XLA Ops:
  0.6 18.5 %copy-start = (f32[8,8,512]{2,1,0:T(8,128)S(1)}, f32[8,8,512]{2,1,0:T(8,128)}, u32[]{:S(2)}) copy-start(f32[8,8,512]{2,1,0:T(8,128)} %param.4) | copy-start | bytes 393220
  1.7 11.7 %collective-permute-start = (f32[8,1,512]{2,1,0:T(1,128)S(1)}, f32[8,1,512]{2,1,0:T(1,128)S(1)}, u32[]{:S(2)}, u32[]{:S(2)}) collective-permute-start(f32[8,1,512]{2,1,0:T(1,128)S(1)} %get-tuple-element.31), channel_id=1, source_target_pairs={{0,4},{4,8},{8,12},{1,5},{5,9},{9,13},{2,6},{6,10},{10,14},{3,7},{... | collective-permute-start | bytes 49160 | tf_op jit(solution)/shard_map/ppermute | solution.py:15
  4.1 20.2 %copy-start.1 = (f32[32,8,512]{2,1,0:T(8,128)S(1)}, f32[32,8,512]{2,1,0:T(8,128)}, u32[]{:S(2)}) copy-start(f32[32,8,512]{2,1,0:T(8,128)} %param.3) | copy-start | bytes 1572868
  4.1 9.3 %collective-permute-start.1 = (f32[8,1,512]{2,1,0:T(1,128)S(1)}, f32[8,1,512]{2,1,0:T(1,128)S(1)}, u32[]{:S(2)}, u32[]{:S(2)}) collective-permute-start(f32[8,1,512]{2,1,0:T(1,128)S(1)} %get-tuple-element.32), channel_id=1, source_target_pairs={{4,0},{8,4},{12,8},{5,1},{9,5},{13,9},{6,2},{10,6},{14,10},{7,3},{... | collective-permute-start | bytes 49160 | tf_op jit(solution)/shard_map/ppermute | solution.py:18
  6.9 17.3 %collective-permute-start.4 = (f32[32,2,512]{2,0,1:T(8,128)S(1)}, f32[32,2,512]{2,0,1:T(8,128)S(1)}, u32[]{:S(2)}, u32[]{:S(2)}) collective-permute-start(f32[32,2,512]{2,0,1:T(8,128)S(1)} %copy.47), channel_id=1, source_target_pairs={{0,4},{4,8},{8,12},{1,5},{5,9},{9,13},{2,6},{6,10},{10,14},{3,7},{... | collective-permute-start | bytes 393224 | tf_op jit(solution)/shard_map/ppermute | solution.py:15
  12.1 12.5 %collective-permute-start.5 = (f32[32,2,512]{2,0,1:T(8,128)S(1)}, f32[32,2,512]{2,0,1:T(8,128)S(1)}, u32[]{:S(2)}, u32[]{:S(2)}) collective-permute-start(f32[32,2,512]{2,0,1:T(8,128)S(1)} %copy.48), channel_id=1, source_target_pairs={{4,0},{8,4},{12,8},{5,1},{9,5},{13,9},{6,2},{10,6},{14,10},{7,3},{... | collective-permute-start | bytes 393224 | tf_op jit(solution)/shard_map/ppermute | solution.py:18
  14.3 5.4 %collective-permute-start.2 = (f32[8,10,1]{2,1,0:T(8,128)S(1)}, f32[8,10,1]{2,1,0:T(8,128)S(1)}, u32[]{:S(2)}, u32[]{:S(2)}) collective-permute-start(f32[8,10,1]{2,1,0:T(8,128)S(1)} %get-tuple-element.21), channel_id=1, source_target_pairs={{0,1},{1,2},{2,3},{4,5},{5,6},{6,7},{8,9},{9,10},{10,11},{12,13},{... | collective-permute-start | bytes 968 | tf_op jit(solution)/shard_map/ppermute | solution.py:15
  17.8 6.2 %collective-permute-start.3 = (f32[8,10,1]{2,1,0:T(8,128)S(1)}, f32[8,10,1]{2,1,0:T(8,128)S(1)}, u32[]{:S(2)}, u32[]{:S(2)}) collective-permute-start(f32[8,10,1]{2,1,0:T(8,128)S(1)} %get-tuple-element.22), channel_id=1, source_target_pairs={{1,0},{2,1},{3,2},{5,4},{6,5},{7,6},{9,8},{10,9},{11,10},{13,12},{... | collective-permute-start | bytes 968 | tf_op jit(solution)/shard_map/ppermute | solution.py:18
  24.8 8.8 %collective-permute-start.6 = (f32[32,12,2]{2,0,1:T(8,128)S(1)}, f32[32,12,2]{2,0,1:T(8,128)S(1)}, u32[]{:S(2)}, u32[]{:S(2)}) collective-permute-start(f32[32,12,2]{2,0,1:T(8,128)S(1)} %get-tuple-element.7), channel_id=1, source_target_pairs={{0,1},{1,2},{2,3},{4,5},{5,6},{6,7},{8,9},{9,10},{10,11},{12,13},{... | collective-permute-start | bytes 9224 | tf_op jit(solution)/shard_map/ppermute | solution.py:15
  28.3 9.3 %collective-permute-start.7 = (f32[32,12,2]{2,0,1:T(8,128)S(1)}, f32[32,12,2]{2,0,1:T(8,128)S(1)}, u32[]{:S(2)}, u32[]{:S(2)}) collective-permute-start(f32[32,12,2]{2,0,1:T(8,128)S(1)} %get-tuple-element.8), channel_id=1, source_target_pairs={{1,0},{2,1},{3,2},{5,4},{6,5},{7,6},{9,8},{10,9},{11,10},{13,12},{... | collective-permute-start | bytes 9224 | tf_op jit(solution)/shard_map/ppermute | solution.py:18
where the time goes:
time: 179 us
  blocking collectives  117 us (65%)
  starting transfers between devices  19.8 us (11%)
  other arithmetic  16.3 us (9%)
  waiting for transfers between devices  12.8 us (7%)
  local copies, waits for them, and re-layouts  6.29 us (4%)
  matrix products  5.25 us (3%)
    psum x2, blocking collectives, factorize(): summed = lax.psum(gram_local, ('row', 'col'))  117 us
    ppermute x4, starting transfers between devices, padded_2(): lax.ppermute(lax.slice_in_dim(block, block.shape[dim] - width, None, axis...  14.5 us
    ppermute x4, waiting for transfers between devices, padded_2(): lax.ppermute(lax.slice_in_dim(block, 0, width, axis=dim), axis, backward)  8.38 us
    another operation x6, other arithmetic, factorize(): return jnp.linalg.cholesky(summed)  7.19 us
    another operation x3, other arithmetic, solve_planes(): jax.scipy.linalg.solve_triangular(lower_tri, image_vals.reshape(columns,...  5.52 us
    ppermute x4, starting transfers between devices, padded_2(): lax.ppermute(lax.slice_in_dim(block, 0, width, axis=dim), axis, backward)  5.3 us
    ppermute x4, waiting for transfers between devices, padded_2(): lax.ppermute(lax.slice_in_dim(block, block.shape[dim] - width, None, axis...  4.46 us
  transfers between devices with their start and end apart: 8, of which 4 were waited for; matrix products, arithmetic and copies ran while one was open for 2% of the time, Pallas kernels for 0%

commit v1 on v0

--- a/solution.py
+++ b/solution.py
@@ -42,7 +42,8 @@
     columns = interior.shape[0]
     flattened = interior.reshape(columns, -1)
     gram_local = jnp.dot(flattened, flattened.T, precision=lax.Precision.HIGHEST) / pixel_count
-    summed = lax.psum(gram_local, ("row", "col"))
+    inner = lax.psum(gram_local, "col")
+    summed = lax.psum(inner, "row")
     return jnp.linalg.cholesky(summed)
 
 

time: 179 us -> 115 us (0.64)
  blocking collectives: 117 us -> 52.9 us
    psum x2 -> x4, blocking collectives: 117 us -> 52.9 us  [the longest x2 32.5 us: factorize(): inner = lax.psum(gram_local, 'col')]
  transfers between devices with their start and end apart: 8 -> 8, of which waited for: 4 -> 4; matrix products, arithmetic and copies ran while one was open for 2% -> 3% of each run, Pallas kernels for 0% -> 0%
where the time goes in v1:
time: 115 us; the launch traced here: 114 us
  blocking collectives  52.9 us (46%)
  starting transfers between devices  19.8 us (17%)
  other arithmetic  16.3 us (14%)
  waiting for transfers between devices  12.8 us (11%)
  local copies, waits for them, and re-layouts  6.3 us (5%)
  matrix products  5.25 us (5%)
    psum x2, blocking collectives, factorize(): inner = lax.psum(gram_local, 'col')  32.5 us
    psum x2, blocking collectives, factorize(): summed = lax.psum(inner, 'row')  20.4 us
    ppermute x4, starting transfers between devices, padded_2(): lax.ppermute(lax.slice_in_dim(block, block.shape[dim] - width, None, axis...  14.5 us
    ppermute x4, waiting for transfers between devices, padded_2(): lax.ppermute(lax.slice_in_dim(block, 0, width, axis=dim), axis, backward)  8.38 us
    another operation x6, other arithmetic, factorize(): return jnp.linalg.cholesky(summed)  7.19 us
    another operation x3, other arithmetic, solve_planes(): jax.scipy.linalg.solve_triangular(lower_tri, image_vals.reshape(columns,...  5.52 us
    ppermute x4, starting transfers between devices, padded_2(): lax.ppermute(lax.slice_in_dim(block, 0, width, axis=dim), axis, backward)  5.3 us
    ppermute x4, waiting for transfers between devices, padded_2(): lax.ppermute(lax.slice_in_dim(block, block.shape[dim] - width, None, axis...  4.46 us
  transfers between devices with their start and end apart: 8, of which 4 were waited for; matrix products, arithmetic and copies ran while one was open for 3% of the time, Pallas kernels for 0%

profile of v1, /device:TPU:0, one launch (start us, length us, event | category | flops | bytes accessed | tf_op | source)
XLA Modules:
  0.0 114.3 jit_solution(15108318546375269612)
XLA Ops:
  0.6 1.1 fusion.45
  1.7 2.4 %collective-permute-start = (f32[8,1,512]{2,1,0:T(1,128)S(1)}, f32[8,1,512]{2,1,0:T(1,128)S(1)}, u32[]{:S(2)}, u32[]{:S(2)}) collective-permute-start(f32[8,1,512]{2,1,0:T(1,128)S(1)} %get-tuple-element.31), channel_id=1, source_target_pairs={{0,4},{4,8},{8,12},{1,5},{5,9},{9,13},{2,6},{6,10},{10,14},{3,7},{... | collective-permute-start | bytes 49160 | tf_op jit(solution)/shard_map/ppermute | solution.py:15
  4.1 1.4 %collective-permute-start.1 = (f32[8,1,512]{2,1,0:T(1,128)S(1)}, f32[8,1,512]{2,1,0:T(1,128)S(1)}, u32[]{:S(2)}, u32[]{:S(2)}) collective-permute-start(f32[8,1,512]{2,1,0:T(1,128)S(1)} %get-tuple-element.32), channel_id=1, source_target_pairs={{4,0},{8,4},{12,8},{5,1},{9,5},{13,9},{6,2},{10,6},{14,10},{7,3},{... | collective-permute-start | bytes 49160 | tf_op jit(solution)/shard_map/ppermute | solution.py:18
  5.5 1.4 %fusion.44 = (f32[32,2,512]{2,1,0:T(2,128)S(1)}, f32[32,2,512]{2,1,0:T(2,128)S(1)}) fusion(f32[32,8,512]{2,1,0:T(8,128)} %param.3), kind=kLoop, calls=%fused_computation.102 | loop fusion | bytes 524288 | tf_op jit(solution)/shard_map/slice | solution.py:18
  6.9 5.1 %collective-permute-start.4 = (f32[32,2,512]{2,0,1:T(8,128)S(1)}, f32[32,2,512]{2,0,1:T(8,128)S(1)}, u32[]{:S(2)}, u32[]{:S(2)}) collective-permute-start(f32[32,2,512]{2,0,1:T(8,128)S(1)} %copy.47), channel_id=1, source_target_pairs={{0,4},{4,8},{8,12},{1,5},{5,9},{9,13},{2,6},{6,10},{10,14},{3,7},{... | collective-permute-start | bytes 393224 | tf_op jit(solution)/shard_map/ppermute | solution.py:15
  12.1 1.3 %collective-permute-start.5 = (f32[32,2,512]{2,0,1:T(8,128)S(1)}, f32[32,2,512]{2,0,1:T(8,128)S(1)}, u32[]{:S(2)}, u32[]{:S(2)}) collective-permute-start(f32[32,2,512]{2,0,1:T(8,128)S(1)} %copy.48), channel_id=1, source_target_pairs={{4,0},{8,4},{12,8},{5,1},{9,5},{13,9},{6,2},{10,6},{14,10},{7,3},{... | collective-permute-start | bytes 393224 | tf_op jit(solution)/shard_map/ppermute | solution.py:18
  13.4 0.9 pad_maximum_fusion.6
  14.3 3.5 %collective-permute-start.2 = (f32[8,10,1]{2,1,0:T(8,128)S(1)}, f32[8,10,1]{2,1,0:T(8,128)S(1)}, u32[]{:S(2)}, u32[]{:S(2)}) collective-permute-start(f32[8,10,1]{2,1,0:T(8,128)S(1)} %get-tuple-element.21), channel_id=1, source_target_pairs={{0,1},{1,2},{2,3},{4,5},{5,6},{6,7},{8,9},{9,10},{10,11},{12,13},{... | collective-permute-start | bytes 968 | tf_op jit(solution)/shard_map/ppermute | solution.py:15
  17.8 1.3 %collective-permute-start.3 = (f32[8,10,1]{2,1,0:T(8,128)S(1)}, f32[8,10,1]{2,1,0:T(8,128)S(1)}, u32[]{:S(2)}, u32[]{:S(2)}) collective-permute-start(f32[8,10,1]{2,1,0:T(8,128)S(1)} %get-tuple-element.22), channel_id=1, source_target_pairs={{1,0},{2,1},{3,2},{5,4},{6,5},{7,6},{9,8},{10,9},{11,10},{13,12},{... | collective-permute-start | bytes 968 | tf_op jit(solution)/shard_map/ppermute | solution.py:18
  19.7 4.3 %collective-permute-done.3 = f32[8,10,1]{2,1,0:T(8,128)S(1)} collective-permute-done((f32[8,10,1]{2,1,0:T(8,128)S(1)}, f32[8,10,1]{2,1,0:T(8,128)S(1)}, u32[]{:S(2)}, u32[]{:S(2)}) %collective-permute-start.3) | collective-permute-done | bytes 352 | tf_op jit(solution)/shard_map/ppermute | solution.py:18
  24.8 3.5 %collective-permute-start.6 = (f32[32,12,2]{2,0,1:T(8,128)S(1)}, f32[32,12,2]{2,0,1:T(8,128)S(1)}, u32[]{:S(2)}, u32[]{:S(2)}) collective-permute-start(f32[32,12,2]{2,0,1:T(8,128)S(1)} %get-tuple-element.7), channel_id=1, source_target_pairs={{0,1},{1,2},{2,3},{4,5},{5,6},{6,7},{8,9},{9,10},{10,11},{12,13},{... | collective-permute-start | bytes 9224 | tf_op jit(solution)/shard_map/ppermute | solution.py:15
  28.3 1.3 %collective-permute-start.7 = (f32[32,12,2]{2,0,1:T(8,128)S(1)}, f32[32,12,2]{2,0,1:T(8,128)S(1)}, u32[]{:S(2)}, u32[]{:S(2)}) collective-permute-start(f32[32,12,2]{2,0,1:T(8,128)S(1)} %get-tuple-element.8), channel_id=1, source_target_pairs={{1,0},{2,1},{3,2},{5,4},{6,5},{7,6},{9,8},{10,9},{11,10},{13,12},{... | collective-permute-start | bytes 9224 | tf_op jit(solution)/shard_map/ppermute | solution.py:18
  29.6 3.9 %collective-permute-done.6 = f32[32,12,2]{2,0,1:T(8,128)S(1)} collective-permute-done((f32[32,12,2]{2,0,1:T(8,128)S(1)}, f32[32,12,2]{2,0,1:T(8,128)S(1)}, u32[]{:S(2)}, u32[]{:S(2)}) %collective-permute-start.6) | collective-permute-done | bytes 3104 | tf_op jit(solution)/shard_map/ppermute | solution.py:15
  33.5 4.1 %collective-permute-done.7 = f32[32,12,2]{2,0,1:T(8,128)S(1)} collective-permute-done((f32[32,12,2]{2,0,1:T(8,128)S(1)}, f32[32,12,2]{2,0,1:T(8,128)S(1)}, u32[]{:S(2)}, u32[]{:S(2)}) %collective-permute-start.7) | collective-permute-done | bytes 3104 | tf_op jit(solution)/shard_map/ppermute | solution.py:18
  38.0 1.4 %fusion.7 = f32[32,10,514]{2,0,1:T(8,128)S(1)} fusion(f32[32,12,512]{2,0,1:T(8,128)S(1)} %constant_dynamic-update-slice_fusion, f32[32,12,2]{2,0,1:T(8,128)S(1)} %collective-permute-done.7, f32[32,12,2]{2,0,1:T(8,128)S(1)} %collective-permute-done.6, f32[32,12,516]{2,0,1:T(8,128)S(1)} %pad_maximum_fusion, f32[10,514]{1,0:T(8,128)S(1)} %get-tuple-element.18, ...), kind=kLoop, calls=%fused_computation.18 | loop fusion | flops 3783040 | bytes 3609296 | tf_op jit(solution)/shard_map/add | solution.py:32
  39.4 0.7 fusion.1
  40.6 17.0 %psum.28 = f32[32,32]{0,1:T(8,128)S(1)} all-reduce(f32[32,32]{0,1:T(8,128)S(1)} %fusion.1), channel_id=1, replica_groups=mesh['sec'=2,'row'=4,'col'=4] {'col'}, use_global_device_ids=true, to_apply=%region_2.0 | all-reduce | flops 1024 | bytes 8192 | tf_op jit(solution)/shard_map/psum | solution.py:45
  57.6 10.1 %psum.29 = f32[32,32]{0,1:T(8,128)S(1)} all-reduce(f32[32,32]{0,1:T(8,128)S(1)} %psum.28), channel_id=1, replica_groups=mesh['sec'=2,'row'=4,'col'=4] {'row'}, use_global_device_ids=true, to_apply=%region_3.4 | all-reduce | flops 1024 | bytes 8192 | tf_op jit(solution)/shard_map/psum | solution.py:46
  67.8 2.9 %cholesky.44 = f32[32,32]{1,0:T(8,128)S(1)} custom-call(f32[32,32]{1,0:T(8,128)S(1)} %fusion.38), custom_call_target="Cholesky" | custom-call | tf_op jit(solution)/shard_map/jit(cholesky)/cholesky | solution.py:47
  70.8 0.6 compare_reduce_fusion.1
  71.4 0.7 fusion.34
  72.1 2.4 %custom-call.10 = f32[1,32,32]{1,2,0:T(8,128)S(1)} custom-call(f32[1,32,32]{2,1,0:T(8,128)S(1)} %fusion.34), custom_call_target="InvertDiagBlocksLowerTriangular" | custom-call | tf_op jit(solution)/shard_map/jit(_solve_triangular)/triangular_solve | solution.py:52
  75.4 1.0 fusion.20
  76.4 2.1 %fusion = f32[32,32]{0,1:T(8,128)S(1)} fusion(f32[32,10,514]{2,0,1:T(8,128)S(1)} %fusion.20, f32[8,512]{1,0:T(8,128)S(1)} %get-tuple-element.29, f32[8,512]{1,0:T(8,128)S(1)} %get-tuple-element.30, f32[8,512]{1,0:T(8,128)S(1)} %get-tuple-element.24, f32[8,512]{1,0:T(8,128)S(1)} %get-tuple-element.25, f32[8,512]{1,0:T(8,128)S(1)} %get-tuple-element.26, ...), kind=kOutput, calls=%fused_computation.5 | convolution fusion | flops 54789120 | bytes 9736192 | tf_op jit(solution)/shard_map/dot_general | solution.py:44
  78.5 15.5 %psum.30 = f32[32,32]{0,1:T(8,128)S(1)} all-reduce(f32[32,32]{0,1:T(8,128)S(1)} %fusion), channel_id=1, replica_groups=mesh['sec'=2,'row'=4,'col'=4] {'col'}, use_global_device_ids=true, to_apply=%region_6.8 | all-reduce | flops 1024 | bytes 8192 | tf_op jit(solution)/shard_map/psum | solution.py:45
  94.0 10.3 %psum.31 = f32[32,32]{0,1:T(8,128)S(1)} all-reduce(f32[32,32]{0,1:T(8,128)S(1)} %psum.30), channel_id=1, replica_groups=mesh['sec'=2,'row'=4,'col'=4] {'row'}, use_global_device_ids=true, to_apply=%region_7.9 | all-reduce | flops 1024 | bytes 8192 | tf_op jit(solution)/shard_map/psum | solution.py:46
  104.4 2.9 %cholesky.55 = f32[32,32]{1,0:T(8,128)S(1)} custom-call(f32[32,32]{1,0:T(8,128)S(1)} %fusion.37), custom_call_target="Cholesky" | custom-call | tf_op jit(solution)/shard_map/jit(cholesky)/cholesky | solution.py:47
  108.0 0.7 fusion.41
  108.6 2.4 %custom-call.11 = f32[1,32,32]{1,2,0:T(8,128)S(1)} custom-call(f32[1,32,32]{2,1,0:T(8,128)S(1)} %get-tuple-element.34), custom_call_target="InvertDiagBlocksLowerTriangular" | custom-call | tf_op jit(solution)/shard_map/jit(_solve_triangular)/triangular_solve | solution.py:52
  111.1 1.4 %fusion.22 = f32[32,8,512]{2,0,1:T(8,128)S(1)} fusion(f32[1,32,32]{1,2,0:T(8,128)S(1)} %custom-call.11, f32[32,10,514]{2,0,1:T(8,128)S(1)} %fusion.20, f32[8,512]{1,0:T(8,128)S(1)} %get-tuple-element.29, f32[8,512]{1,0:T(8,128)S(1)} %get-tuple-element.30, f32[8,512]{1,0:T(8,128)S(1)} %get-tuple-element.24, f32[8,512]{1,0:T(8,128)S(1)} %get-tuple-element.25, ...), kind=kOutput, calls=%fused_computation.38 | convolution fusion | flops 52559872 | bytes 5406720 | tf_op jit(solution)/shard_map/jit(_solve_triangular)/triangular_solve | solution.py:52
  112.5 1.1 copy.28
  113.6 0.7 copy.29
  (30 shorter events, 4.0 us)
Async XLA Ops:
  0.6 18.5 %copy-start = (f32[8,8,512]{2,1,0:T(8,128)S(1)}, f32[8,8,512]{2,1,0:T(8,128)}, u32[]{:S(2)}) copy-start(f32[8,8,512]{2,1,0:T(8,128)} %param.4) | copy-start | bytes 393220
  1.7 11.7 %collective-permute-start = (f32[8,1,512]{2,1,0:T(1,128)S(1)}, f32[8,1,512]{2,1,0:T(1,128)S(1)}, u32[]{:S(2)}, u32[]{:S(2)}) collective-permute-start(f32[8,1,512]{2,1,0:T(1,128)S(1)} %get-tuple-element.31), channel_id=1, source_target_pairs={{0,4},{4,8},{8,12},{1,5},{5,9},{9,13},{2,6},{6,10},{10,14},{3,7},{... | collective-permute-start | bytes 49160 | tf_op jit(solution)/shard_map/ppermute | solution.py:15
  4.1 20.2 %copy-start.1 = (f32[32,8,512]{2,1,0:T(8,128)S(1)}, f32[32,8,512]{2,1,0:T(8,128)}, u32[]{:S(2)}) copy-start(f32[32,8,512]{2,1,0:T(8,128)} %param.3) | copy-start | bytes 1572868
  4.1 9.3 %collective-permute-start.1 = (f32[8,1,512]{2,1,0:T(1,128)S(1)}, f32[8,1,512]{2,1,0:T(1,128)S(1)}, u32[]{:S(2)}, u32[]{:S(2)}) collective-permute-start(f32[8,1,512]{2,1,0:T(1,128)S(1)} %get-tuple-element.32), channel_id=1, source_target_pairs={{4,0},{8,4},{12,8},{5,1},{9,5},{13,9},{6,2},{10,6},{14,10},{7,3},{... | collective-permute-start | bytes 49160 | tf_op jit(solution)/shard_map/ppermute | solution.py:18
  6.9 17.3 %collective-permute-start.4 = (f32[32,2,512]{2,0,1:T(8,128)S(1)}, f32[32,2,512]{2,0,1:T(8,128)S(1)}, u32[]{:S(2)}, u32[]{:S(2)}) collective-permute-start(f32[32,2,512]{2,0,1:T(8,128)S(1)} %copy.47), channel_id=1, source_target_pairs={{0,4},{4,8},{8,12},{1,5},{5,9},{9,13},{2,6},{6,10},{10,14},{3,7},{... | collective-permute-start | bytes 393224 | tf_op jit(solution)/shard_map/ppermute | solution.py:15
  12.1 12.5 %collective-permute-start.5 = (f32[32,2,512]{2,0,1:T(8,128)S(1)}, f32[32,2,512]{2,0,1:T(8,128)S(1)}, u32[]{:S(2)}, u32[]{:S(2)}) collective-permute-start(f32[32,2,512]{2,0,1:T(8,128)S(1)} %copy.48), channel_id=1, source_target_pairs={{4,0},{8,4},{12,8},{5,1},{9,5},{13,9},{6,2},{10,6},{14,10},{7,3},{... | collective-permute-start | bytes 393224 | tf_op jit(solution)/shard_map/ppermute | solution.py:18
  14.3 5.4 %collective-permute-start.2 = (f32[8,10,1]{2,1,0:T(8,128)S(1)}, f32[8,10,1]{2,1,0:T(8,128)S(1)}, u32[]{:S(2)}, u32[]{:S(2)}) collective-permute-start(f32[8,10,1]{2,1,0:T(8,128)S(1)} %get-tuple-element.21), channel_id=1, source_target_pairs={{0,1},{1,2},{2,3},{4,5},{5,6},{6,7},{8,9},{9,10},{10,11},{12,13},{... | collective-permute-start | bytes 968 | tf_op jit(solution)/shard_map/ppermute | solution.py:15
  17.8 6.2 %collective-permute-start.3 = (f32[8,10,1]{2,1,0:T(8,128)S(1)}, f32[8,10,1]{2,1,0:T(8,128)S(1)}, u32[]{:S(2)}, u32[]{:S(2)}) collective-permute-start(f32[8,10,1]{2,1,0:T(8,128)S(1)} %get-tuple-element.22), channel_id=1, source_target_pairs={{1,0},{2,1},{3,2},{5,4},{6,5},{7,6},{9,8},{10,9},{11,10},{13,12},{... | collective-permute-start | bytes 968 | tf_op jit(solution)/shard_map/ppermute | solution.py:18
  24.8 8.8 %collective-permute-start.6 = (f32[32,12,2]{2,0,1:T(8,128)S(1)}, f32[32,12,2]{2,0,1:T(8,128)S(1)}, u32[]{:S(2)}, u32[]{:S(2)}) collective-permute-start(f32[32,12,2]{2,0,1:T(8,128)S(1)} %get-tuple-element.7), channel_id=1, source_target_pairs={{0,1},{1,2},{2,3},{4,5},{5,6},{6,7},{8,9},{9,10},{10,11},{12,13},{... | collective-permute-start | bytes 9224 | tf_op jit(solution)/shard_map/ppermute | solution.py:15
  28.3 9.3 %collective-permute-start.7 = (f32[32,12,2]{2,0,1:T(8,128)S(1)}, f32[32,12,2]{2,0,1:T(8,128)S(1)}, u32[]{:S(2)}, u32[]{:S(2)}) collective-permute-start(f32[32,12,2]{2,0,1:T(8,128)S(1)} %get-tuple-element.8), channel_id=1, source_target_pairs={{1,0},{2,1},{3,2},{5,4},{6,5},{7,6},{9,8},{10,9},{11,10},{13,12},{... | collective-permute-start | bytes 9224 | tf_op jit(solution)/shard_map/ppermute | solution.py:18
